TPU v7x, 32 devices: a whole 2x2x4 slice. The times are simulated.
32 devices in a mesh: chan: 16 (over z, y, core), tm: 2 (over x).
Axes of the slice: x: 2, y: 2, z: 4, core: 2. Of those that a mesh axis runs over, the one named last changes fastest.
Arguments:
- samples: bfloat16 [256, 4096], P('chan', 'tm'), may hold values from -6 to 6
- fir_taps: float32 [96], replicated, may hold values from -0.625 to 0.625
- plan: int32 [4], replicated, may hold values from 1 to 15, as said below
Outputs:
- self_corr: float32 [256, 16, 129], P(('chan', 'tm'))
- pair_corr: float32 [4, 256, 16, 129], P(None, ('chan', 'tm'))
Inputs may be any that keep to these rules, and one draw needn't show every extreme that they name: Round r pairs block g with block g XOR plan[r]; the masks of the rounds are distinct, and the values 1 and 15 both occur.
All inputs are finite; a program needn't handle non-finite values.
Results may differ from a plain program's by a relative error of at most 0.0043.
Values may be sent and summed in bfloat16 or wider, within the bound.
No kernel may reach another device: no remote copies, remote signals or barrier semaphores. Data moves between devices by JAX's collectives and lax.ppermute only.
A program may use at most 128 MiB of HBM per device.

v0:
```python
import math

import jax
import jax.numpy as jnp
from jax import lax
from jax.sharding import PartitionSpec as P

SEGS_DEV = 2
LAGS = 129
ROUNDS = 4


def shifted(x, axis, by):
    devices = lax.axis_size(axis)
    pairs = [(i, i + by) for i in range(devices) if 0 <= i + by < devices]
    return lax.ppermute(x, axis, pairs)


def from_partner(block, axis, distance):
    count = lax.axis_size(axis)
    route = []
    for low in range(count):
        high = low | 1 << distance
        if high != low and high < count:
            route += [(low, high), (high, low)]
    return lax.ppermute(block, axis, route)


def dft_matrix(length, half):
    sample_index = jnp.arange(length, dtype=jnp.int32)[:, None]
    freq_index = jnp.arange(half, dtype=jnp.int32)[None, :]
    angles = 2.0 * math.pi / length * (sample_index * freq_index % length).astype(jnp.float32)
    return jnp.concatenate([jnp.cos(angles), -jnp.sin(angles)], axis=1)


def band_matrix(fir_taps, seg_length):
    tap_count = fir_taps.shape[0]
    window = seg_length + tap_count - 1
    column = jnp.concatenate([fir_taps[::-1], jnp.zeros((window + 1 - tap_count,), jnp.float32)])
    tiled = jnp.tile(column, seg_length)[: seg_length * window]
    return tiled.reshape(seg_length, window).T


def whiten(filtered, matrix):
    spectrum = jnp.dot(
        filtered, matrix, precision=lax.Precision.HIGHEST, preferred_element_type=jnp.float32
    )
    half = matrix.shape[1] // 2
    real_part = spectrum[:, :half]
    imag_part = spectrum[:, half:]
    energy = real_part * real_part + imag_part * imag_part
    water_level = 0.1 * jnp.mean(energy, axis=1, keepdims=True)
    inverse_amp = lax.rsqrt(energy + water_level + 1e-06)
    return jnp.concatenate([real_part * inverse_amp, imag_part * inverse_amp], axis=1).astype(
        jnp.bfloat16
    )


def rotate(spectra, lag_count):
    half = spectra.shape[-1] // 2
    length = 2 * (half - 1)
    lag_value = jnp.arange(lag_count, dtype=jnp.int32) - lag_count // 2
    freq_index = jnp.arange(half, dtype=jnp.int32)
    angles = (
        2.0
        * math.pi
        / length
        * (lag_value[:, None] * freq_index[None, :] % length).astype(jnp.float32)
    )
    edges = (freq_index == 0) | (freq_index == half - 1)
    weight = jnp.where(edges, 1.0, 2.0).astype(jnp.float32) / length
    cosine = jnp.cos(angles) * weight
    sinus = jnp.sin(angles) * weight
    real_part = spectra[..., :half].astype(jnp.float32)[..., None, :]
    imag_part = spectra[..., half:].astype(jnp.float32)[..., None, :]
    rot_real = real_part * cosine - imag_part * sinus
    rot_imag = imag_part * cosine + real_part * sinus
    return jnp.concatenate([rot_real, rot_imag], axis=-1).astype(jnp.bfloat16)


def correlate(rotated, partner):
    return jnp.einsum("salk,sbk->abl", rotated, partner, preferred_element_type=jnp.float32)


def spectra_of(extended, fir_taps, matrix, seg_count, seg_length):
    tap_count = fir_taps.shape[0]
    window = seg_length + tap_count - 1
    chan_count = extended.shape[0]
    widened = extended.astype(jnp.float32)
    windows = jnp.stack(
        [widened[:, s * seg_length : s * seg_length + window] for s in range(seg_count)]
    )
    band = band_matrix(fir_taps, seg_length)
    filtered = jnp.dot(
        windows.reshape(seg_count * chan_count, window),
        band,
        precision=lax.Precision.HIGHEST,
        preferred_element_type=jnp.float32,
    )
    whitened = whiten(filtered, matrix)
    return whitened.reshape(seg_count, chan_count, matrix.shape[1])


def on_device(samples, fir_taps, plan):
    rim_width = fir_taps.shape[0] - 1
    record_length = samples.shape[1]
    seg_count = SEGS_DEV
    seg_length = record_length // seg_count
    before = shifted(samples[:, record_length - rim_width :], "tm", 1)
    extended = jnp.concatenate([before, samples], axis=1)
    matrix = dft_matrix(seg_length, seg_length // 2 + 1)
    own_spectra = spectra_of(extended, fir_taps, matrix, seg_count, seg_length)
    rotated = lax.map(lambda piece: rotate(piece, LAGS), own_spectra)
    self_term = correlate(rotated, own_spectra)
    bit_count = lax.axis_size("chan").bit_length() - 1
    self_corr = lax.psum_scatter(self_term, "tm", scatter_dimension=0, tiled=True)
    stacked = []
    for round_index in range(ROUNDS):
        round_mask = plan[round_index]
        partner = own_spectra
        for bit_index in range(bit_count):
            flag = round_mask >> bit_index & 1 == 1

            def hop_spectra(value, bit_index=bit_index):
                return from_partner(value, "chan", bit_index)

            partner = jnp.where(flag, hop_spectra(partner), partner)
        term = correlate(rotated, partner)
        stacked.append(lax.psum_scatter(term, "tm", scatter_dimension=0, tiled=True))
    pair_corr = jnp.stack(stacked)
    return (self_corr, pair_corr)


def solution(mesh):
    in_specs = (P("chan", "tm"), P(), P())
    out_specs = (P(("chan", "tm"), None, None), P(None, ("chan", "tm"), None, None))
    return jax.shard_map(
        on_device, mesh=mesh, in_specs=in_specs, out_specs=out_specs, check_vma=False
    )
```

profile of v0, /device:TPU:0, one launch (start us, length us, event | category | flops | bytes accessed | tf_op | source)
XLA Modules:
  0.0 183.9 jit_solution(5596529016194202872)
XLA Ops:
  7.2 0.8 slice.42
  8.0 4.8 %collective-permute-start = (bf16[16,95]{1,0:T(8,128)(2,1)S(1)}, bf16[16,95]{1,0:T(8,128)(2,1)S(1)}, u32[]{:S(2)}, u32[]{:S(2)}) collective-permute-start(bf16[16,95]{1,0:T(8,128)(2,1)S(1)} %slice.42), channel_id=1, source_target_pairs={{0,1},{2,3},{4,5},{6,7},{8,9},{10,11},{12,13},{14,15},{16,17},{18,... | collective-permute-start | bytes 9128 | tf_op jit(solution)/shard_map/ppermute | solution.py:16
  12.8 11.3 %sine_negate_fusion = (f32[1024,513]{1,0:T(8,128)S(1)}, f32[1024,513]{1,0:T(8,128)}) fusion(), kind=kLoop, calls=%fused_computation.35 | loop fusion | flops 7879680 | bytes 4202496 | tf_op jit(solution)/shard_map/neg | solution.py:33
  24.1 0.1 rev.3
  24.2 2.5 %tile.4 = f32[1024,1120]{1,0:T(8,128)} broadcast(f32[1120]{0:T(1024)S(1)} %concatenate.37), dimensions={1} | broadcast | bytes 4592000 | tf_op jit(solution)/shard_map/tile | solution.py:40
  26.7 6.4 %tile.10 = f32[1146880]{0:T(1024)} reshape(f32[1024,1120]{1,0:T(8,128)} %tile.4) | data formatting | bytes 9175040 | tf_op jit(solution)/shard_map/tile | solution.py:40
  33.1 3.9 %slice.56 = f32[1145856]{0:T(1024)} slice(f32[1146880]{0:T(1024)} %tile.10), slice={[0:1145856]} | slice | bytes 9166848 | tf_op jit(solution)/shard_map/slice | solution.py:40
  37.1 8.4 %reshape.237 = f32[1024,1119]{1,0:T(8,128)} reshape(f32[1145856]{0:T(1024)} %slice.56) | data formatting | bytes 9166848 | tf_op jit(solution)/shard_map/reshape | solution.py:41
  45.4 0.1 maximum_convert_fusion
  45.6 6.8 %fusion.37 = f32[32,1024]{1,0:T(8,128)S(1)} fusion(f32[32,1119]{1,0:T(8,128)S(1)} %bitcast.91, f32[1024,1119]{1,0:T(8,128)} %reshape.237), kind=kOutput, calls=%fused_computation.84 | convolution fusion | flops 440008704 | bytes 4857728 | tf_op jit(solution)/shard_map/dot_general | solution.py:94
  52.5 2.8 %fusion.10 = f32[32,1026]{1,0:T(8,128)S(1)} fusion(f32[32,1024]{1,0:T(8,128)S(1)} %fusion.37, f32[1024,513]{1,0:T(8,128)S(1)} %get-tuple-element.70, f32[1024,513]{1,0:T(8,128)S(1)} %copy-done), kind=kOutput, calls=%fused_computation.25 | convolution fusion | flops 404490240 | bytes 4464896 | tf_op jit(solution)/shard_map/dot_general | solution.py:45
  55.2 0.2 fusion.35
  55.4 0.1 multiply_convert_fusion.1
  55.5 0.1 pad_maximum_fusion.2
  55.7 0.6 fusion.36
  66.5 0.1 broadcast_select_fusion.9
  66.6 1.6 collective-permute-start.11
  68.2 14.7 %while.12 = (s32[]{:T(128)}, bf16[2,16,129,1026]{3,2,0,1:T(8,128)(2,1)}, bf16[2,16,1026]{2,1,0:T(8,128)(2,1)S(1)}, s32[]{:T(128)}) while((s32[]{:T(128)}, bf16[2,16,129,1026]{3,2,0,1:T(8,128)(2,1)}, bf16[2,16,1026]{2,1,0:T(8,128)(2,1)S(1)}, s32[]{:T(128)}) %tuple.48), condition=%wide.region_2.3_spmd, body=%wide.region_1.2_spmd.sunk | while | flops 18019256 | bytes 14778021 | solution.py:113
  68.2 1.4 cosine_multiply_fusion.2
  69.7 0.1 slice_convert_fusion.3
  69.8 1.7 fusion.48
  71.5 4.1 %fusion.49 = bf16[2,16,129,1026]{3,2,0,1:T(8,128)(2,1)} fusion(bf16[2,16,129,1026]{3,2,0,1:T(8,128)(2,1)} %get-tuple-element.108, s32[]{:T(128)S(6)} %copy.25, bf16[1,16,129,513]{3,2,1,0:T(8,128)(2,1)S(1)} %get-tuple-element.101, bf16[1,16,129,513]{3,2,1,0:T(8,128)(2,1)S(1)} %get-tuple-element.102), kind=kLoop, calls=%fused_computation.3.clone.1 | loop fusion | flops 8470656 | bytes 9248836 | tf_op jit(solution)/shard_map/while/body/jit(dynamic_update_index_in_dim)/dynamic_update_slice | solution.py:113
  75.6 1.4 cosine_multiply_fusion.2
  77.0 0.1 slice_convert_fusion.3
  77.1 1.7 fusion.48
  78.8 4.1 %fusion.49 = bf16[2,16,129,1026]{3,2,0,1:T(8,128)(2,1)} fusion(bf16[2,16,129,1026]{3,2,0,1:T(8,128)(2,1)} %get-tuple-element.108, s32[]{:T(128)S(6)} %copy.25, bf16[1,16,129,513]{3,2,1,0:T(8,128)(2,1)S(1)} %get-tuple-element.101, bf16[1,16,129,513]{3,2,1,0:T(8,128)(2,1)S(1)} %get-tuple-element.102), kind=kLoop, calls=%fused_computation.3.clone.1 | loop fusion | flops 8470656 | bytes 9248836 | tf_op jit(solution)/shard_map/while/body/jit(dynamic_update_index_in_dim)/dynamic_update_slice | solution.py:113
  82.9 0.5 collective-permute-start.8
  83.4 1.5 collective-permute-start.5
  84.9 0.5 collective-permute-start.2
  85.4 1.6 collective-permute-start.12
  87.1 0.9 collective-permute-done.8
  88.0 1.6 collective-permute-start.9
  89.7 1.6 collective-permute-start.6
  91.3 0.8 collective-permute-start.3
  92.1 2.7 %collective-permute-start.13 = (bf16[2,16,1026]{2,1,0:T(8,128)(2,1)S(1)}, bf16[2,16,1026]{2,1,0:T(8,128)(2,1)S(1)}, u32[]{:S(2)}, u32[]{:S(2)}) collective-permute-start(bf16[2,16,1026]{2,1,0:T(8,128)(2,1)S(1)} %broadcast_select_fusion.2), channel_id=1, source_target_pairs={{0,16},{16,0},{2,18},{18,2},{4,20},{20,4},{6,22},{22,6},{8,24},{24... | collective-permute-start | bytes 197000 | tf_op jit(solution)/shard_map/ppermute | solution.py:26
  94.8 0.4 collective-permute-start.10
  95.2 2.7 %collective-permute-start.7 = (bf16[2,16,1026]{2,1,0:T(8,128)(2,1)S(1)}, bf16[2,16,1026]{2,1,0:T(8,128)(2,1)S(1)}, u32[]{:S(2)}, u32[]{:S(2)}) collective-permute-start(bf16[2,16,1026]{2,1,0:T(8,128)(2,1)S(1)} %broadcast_select_fusion.8), channel_id=1, source_target_pairs={{0,16},{16,0},{2,18},{18,2},{4,20},{20,4},{6,22},{22,6},{8,24},{24... | collective-permute-start | bytes 197000 | tf_op jit(solution)/shard_map/ppermute | solution.py:26
  97.9 1.1 collective-permute-start.4
  99.0 3.8 %collective-permute-done.13 = bf16[2,16,1026]{2,1,0:T(8,128)(2,1)S(1)} collective-permute-done((bf16[2,16,1026]{2,1,0:T(8,128)(2,1)S(1)}, bf16[2,16,1026]{2,1,0:T(8,128)(2,1)S(1)}, u32[]{:S(2)}, u32[]{:S(2)}) %collective-permute-start.13) | collective-permute-done | bytes 65696 | tf_op jit(solution)/shard_map/ppermute | solution.py:26
  102.8 7.2 %convolution_bitcast_fusion = f32[16,16,129]{2,1,0:T(8,128)} fusion(bf16[2,16,129,1026]{3,2,0,1:T(8,128)(2,1)} %get-tuple-element.45, bf16[2,16,1026]{2,1,0:T(8,128)(2,1)S(1)} %collective-permute-done.13, bf16[2,16,1026]{2,1,0:T(8,128)(2,1)S(1)} %broadcast_select_fusion.2, pred[]{:T(512)} %bitcast.39), kind=kOutput, calls=%fused_computation.40 | convolution fusion | flops 135563328 | bytes 8734081 | tf_op jit(solution)/shard_map/salk,sbk->abl/dot_general | solution.py:82
  110.1 7.3 %convolution_bitcast_fusion.1 = f32[16,16,129]{2,1,0:T(8,128)} fusion(bf16[2,16,129,1026]{3,2,0,1:T(8,128)(2,1)} %get-tuple-element.45, bf16[2,16,1026]{2,1,0:T(8,128)(2,1)S(1)} %collective-permute-done.10, bf16[2,16,1026]{2,1,0:T(8,128)(2,1)S(1)} %broadcast_select_fusion.5, pred[]{:T(512)} %bitcast.30), kind=kOutput, calls=%fused_computation.41 | convolution fusion | flops 135563328 | bytes 8734081 | tf_op jit(solution)/shard_map/salk,sbk->abl/dot_general | solution.py:82
  117.5 7.3 %convolution_bitcast_fusion.2 = f32[16,16,129]{2,1,0:T(8,128)} fusion(bf16[2,16,129,1026]{3,2,0,1:T(8,128)(2,1)} %get-tuple-element.45, bf16[2,16,1026]{2,1,0:T(8,128)(2,1)S(1)} %collective-permute-done.7, bf16[2,16,1026]{2,1,0:T(8,128)(2,1)S(1)} %broadcast_select_fusion.8, pred[]{:T(512)} %bitcast.21), kind=kOutput, calls=%fused_computation.42 | convolution fusion | flops 135563328 | bytes 8734081 | tf_op jit(solution)/shard_map/salk,sbk->abl/dot_general | solution.py:82
  124.9 7.3 %convolution_bitcast_fusion.3 = f32[16,16,129]{2,1,0:T(8,128)} fusion(bf16[2,16,129,1026]{3,2,0,1:T(8,128)(2,1)} %get-tuple-element.45, bf16[2,16,1026]{2,1,0:T(8,128)(2,1)S(1)} %collective-permute-done.4, bf16[2,16,1026]{2,1,0:T(8,128)(2,1)S(1)} %broadcast_select_fusion.11, pred[]{:T(512)} %bitcast.12), kind=kOutput, calls=%fused_computation.43 | convolution fusion | flops 135563328 | bytes 8734081 | tf_op jit(solution)/shard_map/salk,sbk->abl/dot_general | solution.py:82
  132.2 7.3 %convolution_bitcast_fusion.4 = f32[16,16,129]{2,1,0:T(8,128)} fusion(bf16[2,16,129,1026]{3,2,0,1:T(8,128)(2,1)} %get-tuple-element.45, bf16[2,16,1026]{2,1,0:T(8,128)(2,1)S(1)} %get-tuple-element.121), kind=kOutput, calls=%fused_computation.44 | convolution fusion | flops 135530496 | bytes 8668416 | tf_op jit(solution)/shard_map/salk,sbk->abl/dot_general | solution.py:82
  139.6 9.5 %reduce-scatter.10.cloned.1.call-done = f32[8,16,129]{2,1,0:T(8,128)} async-done(((f32[16,16,129]{2,1,0:T(8,128)}), f32[8,16,129]{2,1,0:T(8,128)}) %reduce-scatter.10.cloned.1.call-update) | async-done | bytes 66064 | tf_op jit(solution)/shard_map/reduce_scatter | solution.py:129
  149.1 13.8 %reduce-scatter.8.cloned.1.call-done = f32[8,16,129]{2,1,0:T(8,128)} async-done(((f32[16,16,129]{2,1,0:T(8,128)}), f32[8,16,129]{2,1,0:T(8,128)}) %reduce-scatter.8.cloned.1.call-update) | async-done | bytes 66064 | tf_op jit(solution)/shard_map/reduce_scatter | solution.py:129
  163.0 1.9 %pad_maximum_fusion = f32[4,8,16,129]{3,2,1,0:T(8,128)} fusion(f32[1,8,16,129]{3,2,1,0:T(8,128)} %bitcast.96, f32[1,8,16,129]{3,2,1,0:T(8,128)} %bitcast.97, f32[1,8,16,129]{3,2,1,0:T(8,128)} %bitcast.98, f32[1,8,16,129]{3,2,1,0:T(8,128)} %bitcast.99), kind=kLoop, calls=%fused_computation.45 | loop fusion | flops 198144 | bytes 528384 | tf_op jit(solution)/shard_map/stack | solution.py:130
  164.9 12.4 %reduce-scatter.6.cloned.1.call-done = f32[8,16,129]{2,1,0:T(8,128)} async-done(((f32[16,16,129]{2,1,0:T(8,128)}), f32[8,16,129]{2,1,0:T(8,128)}) %reduce-scatter.6.cloned.1.call-update) | async-done | bytes 66064 | tf_op jit(solution)/shard_map/reduce_scatter | solution.py:116
  (52 shorter events, 0.6 us)
Async XLA Ops:
  7.2 16.9 %copy-start.3 = (f32[96]{0:T(128)S(1)}, f32[96]{0:T(128)}, u32[]{:S(2)}) copy-start(f32[96]{0:T(128)} %param.6) | copy-start | bytes 1156
  7.2 132.4 %reduce-scatter.14.cloned.1.call-start = ((), (), s32[]{:S(2)}) async-start(), calls=%async_computation.9 | async-start | bytes 393216 | tf_op jit(solution)/shard_map/reduce_scatter | solution.py:129
  8.0 37.5 %collective-permute-start = (bf16[16,95]{1,0:T(8,128)(2,1)S(1)}, bf16[16,95]{1,0:T(8,128)(2,1)S(1)}, u32[]{:S(2)}, u32[]{:S(2)}) collective-permute-start(bf16[16,95]{1,0:T(8,128)(2,1)S(1)} %slice.42), channel_id=1, source_target_pairs={{0,1},{2,3},{4,5},{6,7},{8,9},{10,11},{12,13},{14,15},{16,17},{18,... | collective-permute-start | bytes 9128 | tf_op jit(solution)/shard_map/ppermute | solution.py:16
  37.1 8.4 %copy-start.1 = (bf16[16,2048]{1,0:T(8,128)(2,1)S(1)}, bf16[16,2048]{1,0:T(8,128)(2,1)}, u32[]{:S(2)}) copy-start(bf16[16,2048]{1,0:T(8,128)(2,1)} %param.5) | copy-start | bytes 196612
  45.4 7.0 %copy-start = (f32[1024,513]{1,0:T(8,128)S(1)}, f32[1024,513]{1,0:T(8,128)}, u32[]{:S(2)}) copy-start(f32[1024,513]{1,0:T(8,128)} %get-tuple-element.71) | copy-start | bytes 6303748
  45.6 10.1 %copy-start.2 = (s32[4]{0:T(128)S(1)}, s32[4]{0:T(128)}, u32[]{:S(2)}) copy-start(s32[4]{0:T(128)} %param.7) | copy-start | bytes 52
  55.6 10.9 %collective-permute-start.1 = (bf16[2,16,1026]{2,1,0:T(8,128)(2,1)S(1)}, bf16[2,16,1026]{2,1,0:T(8,128)(2,1)S(1)}, u32[]{:S(2)}, u32[]{:S(2)}) collective-permute-start(bf16[2,16,1026]{2,1,0:T(8,128)(2,1)S(1)} %pad_maximum_fusion.2), channel_id=1, source_target_pairs={{0,2},{2,0},{4,6},{6,4},{8,10},{10,8},{12,14},{14,12},{16,18},{18,... | collective-permute-start | bytes 197000 | tf_op jit(solution)/shard_map/ppermute | solution.py:26
  66.6 18.8 %collective-permute-start.11 = (bf16[2,16,1026]{2,1,0:T(8,128)(2,1)S(1)}, bf16[2,16,1026]{2,1,0:T(8,128)(2,1)S(1)}, u32[]{:S(2)}, u32[]{:S(2)}) collective-permute-start(bf16[2,16,1026]{2,1,0:T(8,128)(2,1)S(1)} %get-tuple-element.61), channel_id=1, source_target_pairs={{0,4},{4,0},{2,6},{6,2},{8,12},{12,8},{10,14},{14,10},{16,20},{20,... | collective-permute-start | bytes 197000 | tf_op jit(solution)/shard_map/ppermute | solution.py:26
  82.9 5.1 %collective-permute-start.8 = (bf16[2,16,1026]{2,1,0:T(8,128)(2,1)S(1)}, bf16[2,16,1026]{2,1,0:T(8,128)(2,1)S(1)}, u32[]{:S(2)}, u32[]{:S(2)}) collective-permute-start(bf16[2,16,1026]{2,1,0:T(8,128)(2,1)S(1)} %get-tuple-element.62), channel_id=1, source_target_pairs={{0,4},{4,0},{2,6},{6,2},{8,12},{12,8},{10,14},{14,10},{16,20},{20,... | collective-permute-start | bytes 197000 | tf_op jit(solution)/shard_map/ppermute | solution.py:26
  83.4 6.3 %collective-permute-start.5 = (bf16[2,16,1026]{2,1,0:T(8,128)(2,1)S(1)}, bf16[2,16,1026]{2,1,0:T(8,128)(2,1)S(1)}, u32[]{:S(2)}, u32[]{:S(2)}) collective-permute-start(bf16[2,16,1026]{2,1,0:T(8,128)(2,1)S(1)} %get-tuple-element.63), channel_id=1, source_target_pairs={{0,4},{4,0},{2,6},{6,2},{8,12},{12,8},{10,14},{14,10},{16,20},{20,... | collective-permute-start | bytes 197000 | tf_op jit(solution)/shard_map/ppermute | solution.py:26
  84.9 6.3 %collective-permute-start.2 = (bf16[2,16,1026]{2,1,0:T(8,128)(2,1)S(1)}, bf16[2,16,1026]{2,1,0:T(8,128)(2,1)S(1)}, u32[]{:S(2)}, u32[]{:S(2)}) collective-permute-start(bf16[2,16,1026]{2,1,0:T(8,128)(2,1)S(1)} %get-tuple-element.60), channel_id=1, source_target_pairs={{0,4},{4,0},{2,6},{6,2},{8,12},{12,8},{10,14},{14,10},{16,20},{20,... | collective-permute-start | bytes 197000 | tf_op jit(solution)/shard_map/ppermute | solution.py:26
  85.4 6.6 %collective-permute-start.12 = (bf16[2,16,1026]{2,1,0:T(8,128)(2,1)S(1)}, bf16[2,16,1026]{2,1,0:T(8,128)(2,1)S(1)}, u32[]{:S(2)}, u32[]{:S(2)}) collective-permute-start(bf16[2,16,1026]{2,1,0:T(8,128)(2,1)S(1)} %broadcast_select_fusion.1), channel_id=1, source_target_pairs={{0,8},{8,0},{2,10},{10,2},{4,12},{12,4},{6,14},{14,6},{16,24},{24,... | collective-permute-start | bytes 197000 | tf_op jit(solution)/shard_map/ppermute | solution.py:26
  88.0 6.8 %collective-permute-start.9 = (bf16[2,16,1026]{2,1,0:T(8,128)(2,1)S(1)}, bf16[2,16,1026]{2,1,0:T(8,128)(2,1)S(1)}, u32[]{:S(2)}, u32[]{:S(2)}) collective-permute-start(bf16[2,16,1026]{2,1,0:T(8,128)(2,1)S(1)} %broadcast_select_fusion.4), channel_id=1, source_target_pairs={{0,8},{8,0},{2,10},{10,2},{4,12},{12,4},{6,14},{14,6},{16,24},{24,... | collective-permute-start | bytes 197000 | tf_op jit(solution)/shard_map/ppermute | solution.py:26
  89.7 5.5 %collective-permute-start.6 = (bf16[2,16,1026]{2,1,0:T(8,128)(2,1)S(1)}, bf16[2,16,1026]{2,1,0:T(8,128)(2,1)S(1)}, u32[]{:S(2)}, u32[]{:S(2)}) collective-permute-start(bf16[2,16,1026]{2,1,0:T(8,128)(2,1)S(1)} %broadcast_select_fusion.7), channel_id=1, source_target_pairs={{0,8},{8,0},{2,10},{10,2},{4,12},{12,4},{6,14},{14,6},{16,24},{24,... | collective-permute-start | bytes 197000 | tf_op jit(solution)/shard_map/ppermute | solution.py:26
  91.3 6.6 %collective-permute-start.3 = (bf16[2,16,1026]{2,1,0:T(8,128)(2,1)S(1)}, bf16[2,16,1026]{2,1,0:T(8,128)(2,1)S(1)}, u32[]{:S(2)}, u32[]{:S(2)}) collective-permute-start(bf16[2,16,1026]{2,1,0:T(8,128)(2,1)S(1)} %broadcast_select_fusion.10), channel_id=1, source_target_pairs={{0,8},{8,0},{2,10},{10,2},{4,12},{12,4},{6,14},{14,6},{16,24},{24,... | collective-permute-start | bytes 197000 | tf_op jit(solution)/shard_map/ppermute | solution.py:26
  92.1 10.7 %collective-permute-start.13 = (bf16[2,16,1026]{2,1,0:T(8,128)(2,1)S(1)}, bf16[2,16,1026]{2,1,0:T(8,128)(2,1)S(1)}, u32[]{:S(2)}, u32[]{:S(2)}) collective-permute-start(bf16[2,16,1026]{2,1,0:T(8,128)(2,1)S(1)} %broadcast_select_fusion.2), channel_id=1, source_target_pairs={{0,16},{16,0},{2,18},{18,2},{4,20},{20,4},{6,22},{22,6},{8,24},{24... | collective-permute-start | bytes 197000 | tf_op jit(solution)/shard_map/ppermute | solution.py:26
  94.8 15.3 %collective-permute-start.10 = (bf16[2,16,1026]{2,1,0:T(8,128)(2,1)S(1)}, bf16[2,16,1026]{2,1,0:T(8,128)(2,1)S(1)}, u32[]{:S(2)}, u32[]{:S(2)}) collective-permute-start(bf16[2,16,1026]{2,1,0:T(8,128)(2,1)S(1)} %broadcast_select_fusion.5), channel_id=1, source_target_pairs={{0,16},{16,0},{2,18},{18,2},{4,20},{20,4},{6,22},{22,6},{8,24},{24... | collective-permute-start | bytes 197000 | tf_op jit(solution)/shard_map/ppermute | solution.py:26
  95.2 22.3 %collective-permute-start.7 = (bf16[2,16,1026]{2,1,0:T(8,128)(2,1)S(1)}, bf16[2,16,1026]{2,1,0:T(8,128)(2,1)S(1)}, u32[]{:S(2)}, u32[]{:S(2)}) collective-permute-start(bf16[2,16,1026]{2,1,0:T(8,128)(2,1)S(1)} %broadcast_select_fusion.8), channel_id=1, source_target_pairs={{0,16},{16,0},{2,18},{18,2},{4,20},{20,4},{6,22},{22,6},{8,24},{24... | collective-permute-start | bytes 197000 | tf_op jit(solution)/shard_map/ppermute | solution.py:26
  97.9 27.0 %collective-permute-start.4 = (bf16[2,16,1026]{2,1,0:T(8,128)(2,1)S(1)}, bf16[2,16,1026]{2,1,0:T(8,128)(2,1)S(1)}, u32[]{:S(2)}, u32[]{:S(2)}) collective-permute-start(bf16[2,16,1026]{2,1,0:T(8,128)(2,1)S(1)} %broadcast_select_fusion.11), channel_id=1, source_target_pairs={{0,16},{16,0},{2,18},{18,2},{4,20},{20,4},{6,22},{22,6},{8,24},{24... | collective-permute-start | bytes 197000 | tf_op jit(solution)/shard_map/ppermute | solution.py:26
  110.1 29.6 %reduce-scatter.12.cloned.1.call-start = ((), (), s32[]{:S(2)}) async-start(), calls=%async_computation.8 | async-start | bytes 393216 | tf_op jit(solution)/shard_map/reduce_scatter | solution.py:129
  117.4 31.7 %reduce-scatter.10.cloned.1.call-start = ((), (), s32[]{:S(2)}) async-start(), calls=%async_computation.7 | async-start | bytes 393216 | tf_op jit(solution)/shard_map/reduce_scatter | solution.py:129
  124.8 38.2 %reduce-scatter.8.cloned.1.call-start = ((), (), s32[]{:S(2)}) async-start(), calls=%async_computation.6 | async-start | bytes 393216 | tf_op jit(solution)/shard_map/reduce_scatter | solution.py:129
  132.2 45.2 %reduce-scatter.6.cloned.1.call-start = ((), (), s32[]{:S(2)}) async-start(), calls=%async_computation.5 | async-start | bytes 393216 | tf_op jit(solution)/shard_map/reduce_scatter | solution.py:116
Sparse Core Ops, SparseCore 0:
  110.2 10.9 reduce-scatter.13
  123.5 11.6 reduce-scatter.11
  137.4 11.6 reduce-scatter.9
  151.3 11.6 reduce-scatter.7
  165.6 11.6 reduce-scatter.5
where the time goes:
time: 185 us; the launch traced here: 184 us
  matrix products  46 us (25%)
  waiting for transfers between devices  40.7 us (22%)
  other arithmetic  28.5 us (15%)
  between operations  24.1 us (13%)
  local copies, waits for them, and re-layouts  22.8 us (12%)
  starting transfers between devices  21.7 us (12%)
    dot_general x5, matrix products, correlate(): jnp.einsum('salk,sbk->abl', rotated, partner, preferred_element_type=jnp....  36.4 us
    reduce_scatter x4, waiting for transfers between devices, on_device(): lax.psum_scatter(term, 'tm', scatter_dimension=0, tiled=True)  23.4 us
    ppermute x13, starting transfers between devices, from_partner(): return lax.ppermute(block, axis, route)  16.7 us
    reduce_scatter x1, waiting for transfers between devices, on_device(): lax.psum_scatter(self_term, 'tm', scatter_dimension=0, tiled=True)  12.4 us
    neg x1, other arithmetic, dft_matrix(): return jnp.concatenate([jnp.cos(angles), -jnp.sin(angles)], axis=1)  11.3 us
    another operation x2, local copies, waits for them, and re-layouts, band_matrix(): tiled = jnp.tile(column, seg_length)[:seg_length * window]  8.94 us
    reshape x1, local copies, waits for them, and re-layouts, band_matrix(): return tiled.reshape(seg_length, window).T  8.37 us
    dynamic_update_slice x2, other arithmetic, on_device(): rotated = lax.map(lambda piece: rotate(piece, LAGS), own_spectra)  8.14 us
  transfers between devices with their start and end apart: 19, of which 5 were waited for; matrix products, arithmetic and copies ran while one was open for 47% of the time, Pallas kernels for 0%

commit v1 on v0

v1 whole, which is shorter than its diff:
```python
import functools
import math

import jax
import jax.numpy as jnp
import ml_dtypes
import numpy as np
from jax import lax
from jax.experimental import pallas as pl
from jax.experimental.pallas import tpu as pltpu
from jax.sharding import PartitionSpec as P

SEGS_DEV = 2
LAGS = 129
ROUNDS = 4
LANE = 128


def split_table(table):
    high = table.astype(ml_dtypes.bfloat16)
    low = (table - high.astype(np.float64)).astype(ml_dtypes.bfloat16)
    return high, low


def tables(length):
    half = length // 2
    quarter = length // 4
    sample = np.arange(half)[:, None]

    def columns(freqs):
        angle = 2.0 * math.pi / length * (sample * freqs[None, :] % length)
        return np.cos(angle), -np.sin(angle)

    even = 2 * np.arange(quarter)
    odd = even + 1
    even_re, even_im = columns(even)
    even_im[:, 0] = 1.0 - 2.0 * (np.arange(half) % 2)
    odd_re, odd_im = columns(odd)
    even_table = np.concatenate([even_re, even_im], axis=1)
    odd_table = np.concatenate([odd_re, odd_im], axis=1)

    freqs = np.concatenate([even, odd])[:, None]
    lag = (np.arange(LAGS) - LAGS // 2)[None, :]
    angle = 2.0 * math.pi / length * (lag * freqs % length)
    weight = np.where(freqs == 0, 1.0, 2.0) / length
    lag_cos = weight * np.cos(angle)
    lag_sin = weight * np.sin(angle)
    lag_sin[0] = (1.0 - 2.0 * (np.abs(lag[0]) % 2)) / length
    lag_table = np.zeros((length, 2 * LANE))
    lag_table[:, :LAGS] = np.concatenate([lag_cos, lag_sin], axis=0)
    return (
        *split_table(even_table),
        *split_table(odd_table),
        lag_table.astype(ml_dtypes.bfloat16),
    )


def dot(left, right):
    return jnp.dot(left, right, preferred_element_type=jnp.float32)


def correlate_kernel(
    parts,
    info,
    own,
    part_0,
    part_1,
    part_2,
    part_3,
    taps,
    even_hi,
    even_lo,
    odd_hi,
    odd_lo,
    lag_table,
    mine,
    others,
    sums,
    diffs,
    real_ref,
    imag_ref,
    left_ref,
    cross,
    result,
):
    blocks = (own, part_0, part_1, part_2, part_3)
    chans = own.shape[0]
    rows_blk = SEGS_DEV * chans
    rows = rows_blk * len(blocks)
    half = even_hi.shape[0]
    quarter = half // 2
    pieces = half // LANE

    base = jnp.broadcast_to(taps[...], (2 * LANE, 2 * LANE))
    toeplitz = pltpu.roll(base, LANE, 1, stride=1, stride_axis=0)[:, :LANE]
    toep_hi = toeplitz.astype(jnp.bfloat16)
    toep_lo = (toeplitz - toep_hi.astype(jnp.float32)).astype(jnp.bfloat16)
    toep = jnp.concatenate([toep_hi, toep_lo], axis=1)

    for q, block in enumerate(blocks):
        windows = jnp.concatenate(
            [block[:, LANE * k : LANE * (k + 2)] for k in range(2 * pieces * SEGS_DEV)], axis=0
        )
        both = dot(windows, toep)
        filtered = both[:, :LANE] + both[:, LANE:]
        for s in range(SEGS_DEV):
            row = q * rows_blk + s * chans
            for k in range(pieces):
                lo = (s * 2 * pieces + k) * chans
                hi = lo + pieces * chans
                first, second = filtered[lo : lo + chans], filtered[hi : hi + chans]
                for ref, value in ((sums, first + second), (diffs, first - second)):
                    high = value.astype(jnp.bfloat16)
                    low = (value - high.astype(jnp.float32)).astype(jnp.bfloat16)
                    ref[row : row + chans, LANE * k : LANE * (k + 1)] = high
                    ref[rows + row : rows + row + chans, LANE * k : LANE * (k + 1)] = low

    def transform(values, table_hi, table_lo):
        main = dot(values[...], table_hi[...])
        return main[:rows] + main[rows:] + dot(values[:rows, :], table_lo[...])

    even = transform(sums, even_hi, even_lo)
    odd = transform(diffs, odd_hi, odd_lo)
    real = jnp.concatenate([even[:, :quarter], odd[:, :quarter]], axis=1)
    imag = jnp.concatenate([even[:, quarter:], odd[:, quarter:]], axis=1)
    edge = lax.broadcasted_iota(jnp.int32, real.shape, 1) == 0
    real_sq = real * real
    imag_sq = imag * imag
    level = 0.1 / (half + 1) * jnp.sum(real_sq + imag_sq, axis=1, keepdims=True) + 1e-06
    inv_real = lax.rsqrt(real_sq + jnp.where(edge, 0.0, imag_sq) + level)
    inv_imag = jnp.where(edge, lax.rsqrt(imag_sq + level), inv_real)
    real = (real * inv_real).astype(jnp.bfloat16).astype(jnp.float32)
    imag = (imag * inv_imag).astype(jnp.bfloat16).astype(jnp.float32)
    real_ref[...] = real
    imag_ref[...] = imag
    lefts = (real, jnp.where(edge, 0.0, imag), jnp.where(edge, imag, real))
    for a in range(chans):
        for s in range(SEGS_DEV):
            row = s * chans + a
            for j, value in enumerate(lefts):
                at = SEGS_DEV * j + s
                left_ref[a, at : at + 1, :] = value[row : row + 1]

    out_rows = chans * len(blocks)

    @pl.loop(0, chans)
    def _(a):
        at = pl.multiple_of(a * out_rows, out_rows)
        for c in range(pieces):
            cols = slice(LANE * c, LANE * (c + 1))
            left = [
                jnp.broadcast_to(left_ref[a, j : j + 1, cols], (chans, LANE))
                for j in range(3 * SEGS_DEV)
            ]
            for q in range(len(blocks)):
                cos_part = sin_part = 0.0
                for s in range(SEGS_DEV):
                    row_b = slice(q * rows_blk + s * chans, q * rows_blk + (s + 1) * chans)
                    re_b, im_b = real_ref[row_b, cols], imag_ref[row_b, cols]
                    re_a, im_a, x_a = (left[SEGS_DEV * j + s] for j in range(3))
                    cos_part += re_a * re_b + im_a * im_b
                    sin_part += x_a * im_b - im_a * re_b
                at_q = pl.ds(at + q * chans, chans)
                cross[at_q, cols] = cos_part.astype(jnp.bfloat16)
                cross[at_q, half + LANE * c : half + LANE * (c + 1)] = sin_part.astype(jnp.bfloat16)

    result[...] = dot(cross[...], lag_table[...])

    place = info[0]
    share = chans // parts
    for j in range(parts):
        owner = lax.rem(place + j, parts)

        @pl.loop(0, share)
        def _(i, j=j, owner=owner):
            at = pl.multiple_of((owner * share + i) * out_rows, out_rows)
            for q in range(len(blocks)):
                slot = 0 if q == 0 else info[q]
                value = result[pl.ds(at + q * chans, chans), :LAGS]
                if j == 0:
                    mine[slot, i] = value
                else:
                    others[j - 1, slot, i] = value.astype(jnp.bfloat16)


def correlate(info, own, partners, fir_taps, parts):
    chans = own.shape[0]
    length = (own.shape[1] - LANE) // SEGS_DEV
    half = length // 2
    sets = ROUNDS + 1
    rows = sets * SEGS_DEV * chans
    taps = jnp.pad(fir_taps, (0, 2 * LANE - fir_taps.shape[0]))[None]
    vmem = pl.BlockSpec(memory_space=pltpu.VMEM)
    smem = pl.BlockSpec(memory_space=pltpu.SMEM)
    share = chans // parts
    return pl.pallas_call(
        functools.partial(correlate_kernel, parts),
        out_shape=(
            jax.ShapeDtypeStruct((sets, share, chans, LAGS), jnp.float32),
            jax.ShapeDtypeStruct((parts - 1, sets, share, chans, LAGS), jnp.bfloat16),
        ),
        in_specs=[smem] + [vmem] * 11,
        out_specs=(vmem, vmem),
        scratch_shapes=[
            pltpu.VMEM((2 * rows, half), jnp.bfloat16),
            pltpu.VMEM((2 * rows, half), jnp.bfloat16),
            pltpu.VMEM((rows, half), jnp.float32),
            pltpu.VMEM((rows, half), jnp.float32),
            pltpu.VMEM((chans, 3 * SEGS_DEV, half), jnp.float32),
            pltpu.VMEM((sets * chans * chans, length), jnp.bfloat16),
            pltpu.VMEM((sets * chans * chans, 2 * LANE), jnp.float32),
        ],
        compiler_params=pltpu.CompilerParams(vmem_limit_bytes=32 * 1024 * 1024),
    )(info, own, *partners, taps, *tables(length))


def from_partner(block, axis, mask):
    count = lax.axis_size(axis)
    return lax.ppermute(block, axis, [(i, i ^ mask) for i in range(count)])


def on_device(samples, fir_taps, plan):
    chan_count = lax.axis_size("chan")
    parts = lax.axis_size("tm")
    tail = samples[:, samples.shape[1] - LANE :]
    before = lax.ppermute(tail, "tm", [(i, i + 1) for i in range(parts - 1)])
    own = jnp.concatenate([before, samples], axis=1)

    fixed_masks = (1, chan_count - 1)
    free_masks = range(2, chan_count - 1)
    masks = [plan[r] for r in range(ROUNDS)]
    seen = jnp.int32(0)
    slots = [jnp.int32(0)] * ROUNDS
    free = [jnp.int32(0)] * 2
    for r, mask in enumerate(masks):
        is_first, is_last = mask == fixed_masks[0], mask == fixed_masks[1]
        is_free = ~(is_first | is_last)
        takes = [is_first, is_last, is_free & (seen == 0), is_free & (seen == 1)]
        slots = [jnp.where(take, r + 1, slot) for take, slot in zip(takes, slots)]
        free = [jnp.where(take, mask, old) for take, old in zip(takes[2:], free)]
        seen = seen + is_free.astype(jnp.int32)

    partners = [from_partner(own, "chan", mask) for mask in fixed_masks]
    routes = [functools.partial(from_partner, axis="chan", mask=mask) for mask in free_masks]
    for mask in free:
        partners.append(lax.switch(mask - free_masks[0], routes, own))

    info = jnp.stack([lax.axis_index("tm").astype(jnp.int32), *slots])
    mine, others = correlate(info, own, partners, fir_taps, parts)
    total = mine
    for j in range(1, parts):
        route = [(i, (i + j) % parts) for i in range(parts)]
        total = total + lax.ppermute(others[j - 1], "tm", route).astype(jnp.float32)
    return total[0], total[1:]


def solution(mesh):
    in_specs = (P("chan", "tm"), P(), P())
    out_specs = (P(("chan", "tm"), None, None), P(None, ("chan", "tm"), None, None))
    return jax.shard_map(
        on_device, mesh=mesh, in_specs=in_specs, out_specs=out_specs, check_vma=False
    )
```

time: 185 us -> 56.1 us (0.30)
  matrix products: 46 us -> 0 us
  other arithmetic: 28.5 us -> 0.1 us
  waiting for transfers between devices: 40.7 us -> 18.8 us
  between operations: 24.1 us -> 10.3 us
  local copies, waits for them, and re-layouts: 22.8 us -> 9.63 us
  starting transfers between devices: 21.7 us -> 12.1 us
  Pallas kernels: 0 us -> 4.97 us
    dot_general x7 -> x0, matrix products: 46 us -> none  [the longest x5 36.4 us: correlate(): jnp.einsum('salk,sbk->abl', rotated, partner, preferred_element_type=jnp....]
    reduce_scatter x5 -> x0, waiting for transfers between devices: 35.8 us -> none  [the longest x4 23.4 us: on_device(): lax.psum_scatter(term, 'tm', scatter_dimension=0, tiled=True)]
    ppermute x14 -> x6, waiting for transfers between devices: 4.75 us -> 18.8 us  [the longest x4 10.7 us: from_partner(): return lax.ppermute(block, axis, [(i, i ^ mask) for i in range(count)])]
    neg x1 -> x0, other arithmetic: 11.3 us -> none  [dft_matrix(): return jnp.concatenate([jnp.cos(angles), -jnp.sin(angles)], axis=1)]
    ppermute x14 -> x6, starting transfers between devices: 21.5 us -> 12.1 us  [the longest x4 4.92 us: from_partner(): return lax.ppermute(block, axis, [(i, i ^ mask) for i in range(count)])]
    another operation x3 -> x1, local copies, waits for them, and re-layouts: 8.95 us -> 0.08 us  [on_device(): info = jnp.stack([lax.axis_index('tm').astype(jnp.int32), *slots])]
    reshape x1 -> x0, local copies, waits for them, and re-layouts: 8.37 us -> none  [band_matrix(): return tiled.reshape(seg_length, window).T]
    dynamic_update_slice x2 -> x0, other arithmetic: 8.14 us -> none  [on_device(): rotated = lax.map(lambda piece: rotate(piece, LAGS), own_spectra)]
  transfers between devices with their start and end apart: 19 -> 6, of which waited for: 5 -> 4; matrix products, arithmetic and copies ran while one was open for 47% -> 1% of each run, Pallas kernels for 0% -> 0%
where the time goes in v1:
time: 56.1 us; the launch traced here: 55.9 us
  waiting for transfers between devices  18.8 us (34%)
  starting transfers between devices  12.1 us (22%)
  between operations  10.3 us (18%)
  local copies, waits for them, and re-layouts  9.63 us (17%)
  Pallas kernels  4.97 us (9%)
    ppermute x4, waiting for transfers between devices, from_partner(): return lax.ppermute(block, axis, [(i, i ^ mask) for i in range(count)])  10.7 us
    ppermute x1, waiting for transfers between devices, on_device(): total = total + lax.ppermute(others[j - 1], 'tm', route).astype(jnp.float32)  6.73 us
    unnamed x15, local copies, waits for them, and re-layouts  5.85 us
    pallas_call x1, Pallas kernels, correlate(): pl.pallas_call(functools.partial(correlate_kernel, parts), out_shape=(jax...  4.97 us
    ppermute x4, starting transfers between devices, from_partner(): return lax.ppermute(block, axis, [(i, i ^ mask) for i in range(count)])  4.92 us
    ppermute x1, starting transfers between devices, on_device(): before = lax.ppermute(tail, 'tm', [(i, i + 1) for i in range(parts - 1)])  4.83 us
    ppermute x1, starting transfers between devices, on_device(): total = total + lax.ppermute(others[j - 1], 'tm', route).astype(jnp.float32)  2.34 us
    ppermute x1, waiting for transfers between devices, on_device(): before = lax.ppermute(tail, 'tm', [(i, i + 1) for i in range(parts - 1)])  1.31 us
  transfers between devices with their start and end apart: 6, of which 4 were waited for; matrix products, arithmetic and copies ran while one was open for 1% of the time, Pallas kernels for 0%

profile of v1, /device:TPU:0, one launch (start us, length us, event | category | flops | bytes accessed | tf_op | source)
XLA Modules:
  0.0 55.9 jit_solution(3202215585055366132)
XLA Ops:
  0.6 0.7 %slice.25 = bf16[16,128]{1,0:T(8,128)(2,1)S(1)} slice(bf16[16,2048]{1,0:T(8,128)(2,1)} %param.34), slice={[0:16], [1920:2048]} | slice | bytes 8192 | tf_op jit(solution)/shard_map/slice | solution.py:225
  1.3 4.8 %collective-permute-start.26 = (bf16[16,128]{1,0:T(8,128)(2,1)S(1)}, bf16[16,128]{1,0:T(8,128)(2,1)S(1)}, u32[]{:S(2)}, u32[]{:S(2)}) collective-permute-start(bf16[16,128]{1,0:T(8,128)(2,1)S(1)} %slice.25), channel_id=1, source_target_pairs={{0,1},{2,3},{4,5},{6,7},{8,9},{10,11},{12,13},{14,15},{16,17},{18,... | collective-permute-start | bytes 12296 | tf_op jit(solution)/shard_map/ppermute | solution.py:226
  6.2 1.3 %collective-permute-done.26 = bf16[16,128]{1,0:T(8,128)(2,1)S(1)} collective-permute-done((bf16[16,128]{1,0:T(8,128)(2,1)S(1)}, bf16[16,128]{1,0:T(8,128)(2,1)S(1)}, u32[]{:S(2)}, u32[]{:S(2)}) %collective-permute-start.26) | collective-permute-done | bytes 4128 | tf_op jit(solution)/shard_map/ppermute | solution.py:226
  7.5 0.0 copy-start.5
  7.5 0.9 %constant_dynamic-update-slice_fusion.own = bf16[16,2176]{1,0:T(8,128)(2,1)S(1)} fusion(bf16[16,2176]{1,0:T(8,128)(2,1)S(1)} %constant_dynamic-update-slice_fusion.1, bf16[16,2048]{1,0:T(8,128)(2,1)} %param.34), kind=kLoop, calls=%fused_computation.2 | loop fusion | bytes 131072 | tf_op jit(solution)/shard_map/concatenate | solution.py:227
  8.3 3.1 %collective-permute-start.28 = (bf16[16,2176]{1,0:T(8,128)(2,1)S(1)}, bf16[16,2176]{1,0:T(8,128)(2,1)S(1)}, u32[]{:S(2)}, u32[]{:S(2)}) collective-permute-start(bf16[16,2176]{1,0:T(8,128)(2,1)S(1)} %constant_dynamic-update-slice_fusion.own), channel_id=1, source_target_pairs={{0,30},{2,28},{4,26},{6,24},{8,22},{10,20},{12,18},{14,16},{16,14}... | collective-permute-start | bytes 208904 | tf_op jit(solution)/shard_map/ppermute | solution.py:219
  11.5 1.5 %collective-permute-start.27 = (bf16[16,2176]{1,0:T(8,128)(2,1)S(1)}, bf16[16,2176]{1,0:T(8,128)(2,1)S(1)}, u32[]{:S(2)}, u32[]{:S(2)}) collective-permute-start(bf16[16,2176]{1,0:T(8,128)(2,1)S(1)} %constant_dynamic-update-slice_fusion.own), channel_id=1, source_target_pairs={{0,2},{2,0},{4,6},{6,4},{8,10},{10,8},{12,14},{14,12},{16,18},{18,... | collective-permute-start | bytes 208904 | tf_op jit(solution)/shard_map/ppermute | solution.py:219
  13.0 0.0 copy-done.5
  13.0 0.6 %fusion = (s32[1]{0:T(128)}, s32[1]{0:T(128)}, s32[1]{0:T(128)}, s32[1]{0:T(128)}) fusion(s32[4]{0:T(128)S(1)} %copy-done.5), kind=kLoop, calls=%fused_computation.4 | loop fusion | bytes 32 | tf_op jit(solution)/shard_map/slice | solution.py:231
  23.3 0.0 copy-start.6
  23.3 0.6 %copy-done.6 = f32[96]{0:T(128)S(1)} copy-done((f32[96]{0:T(128)S(1)}, f32[96]{0:T(128)}, u32[]{:S(2)}) %copy-start.6) | copy-done | bytes 408
  23.9 0.1 stack.23.info
  24.0 6.2 %conditional.3 = (bf16[16,2176]{1,0:T(8,128)(2,1)}) conditional(s32[]{:T(128)} %clamp.7, bf16[16,2176]{1,0:T(8,128)(2,1)S(1)} %constant_dynamic-update-slice_fusion.own, bf16[16,2176]{1,0:T(8,128)(2,1)S(1)} %constant_dynamic-update-slice_fusion.own, ...), branch_computations={%region_13.14_spmd, %region_14.15_spmd, %region_15.16_spmd, %regio... | conditional | bytes 278576 | solution.py:246
  24.0 0.2 collective-permute-start.23
  24.3 6.0 %collective-permute-done.23 = bf16[16,2176]{1,0:T(8,128)(2,1)} collective-permute-done((bf16[16,2176]{1,0:T(8,128)(2,1)S(1)}, bf16[16,2176]{1,0:T(8,128)(2,1)}, u32[]{:S(2)}, u32[]{:S(2)}) %collective-permute-start.23) | collective-permute-done | bytes 69664 | tf_op jit(solution)/shard_map/cond/branch_10_fun/ppermute | solution.py:219
  30.3 4.7 %conditional.2 = (bf16[16,2176]{1,0:T(8,128)(2,1)}) conditional(s32[]{:T(128)} %clamp.6, bf16[16,2176]{1,0:T(8,128)(2,1)S(1)} %constant_dynamic-update-slice_fusion.own, bf16[16,2176]{1,0:T(8,128)(2,1)S(1)} %constant_dynamic-update-slice_fusion.own, ...), branch_computations={%region_0.1_spmd, %region_1.2_spmd, %region_2.3_spmd, %region_3.4_... | conditional | bytes 278576 | solution.py:246
  30.3 0.0 collective-permute-start.5
  30.3 4.7 %collective-permute-done.5 = bf16[16,2176]{1,0:T(8,128)(2,1)} collective-permute-done((bf16[16,2176]{1,0:T(8,128)(2,1)S(1)}, bf16[16,2176]{1,0:T(8,128)(2,1)}, u32[]{:S(2)}, u32[]{:S(2)}) %collective-permute-start.5) | collective-permute-done | bytes 69664 | tf_op jit(solution)/shard_map/cond/branch_5_fun/ppermute | solution.py:219
  35.0 0.0 collective-permute-done.28.part_1
  35.0 0.0 collective-permute-done.27.part_0
  35.0 0.0 copy-start
  35.0 1.0 %copy-done = bf16[1024,256]{1,0:T(8,128)(2,1)S(1)} copy-done((bf16[1024,256]{1,0:T(8,128)(2,1)S(1)}, bf16[1024,256]{1,0:T(8,128)(2,1)}, u32[]{:S(2)}) %copy-start) | copy-done | bytes 524312
  36.1 0.0 copy-start.1
  36.1 1.0 %copy-done.1 = bf16[512,512]{1,0:T(8,128)(2,1)S(1)} copy-done((bf16[512,512]{1,0:T(8,128)(2,1)S(1)}, bf16[512,512]{1,0:T(8,128)(2,1)}, u32[]{:S(2)}) %copy-start.1) | copy-done | bytes 524312
  37.1 0.0 copy-start.2
  37.1 1.0 %copy-done.2 = bf16[512,512]{1,0:T(8,128)(2,1)S(1)} copy-done((bf16[512,512]{1,0:T(8,128)(2,1)S(1)}, bf16[512,512]{1,0:T(8,128)(2,1)}, u32[]{:S(2)}) %copy-start.2) | copy-done | bytes 524312
  38.1 0.0 copy-start.3
  38.1 1.0 %copy-done.3 = bf16[512,512]{1,0:T(8,128)(2,1)S(1)} copy-done((bf16[512,512]{1,0:T(8,128)(2,1)S(1)}, bf16[512,512]{1,0:T(8,128)(2,1)}, u32[]{:S(2)}) %copy-start.3) | copy-done | bytes 524312
  39.2 0.0 copy-start.4
  39.2 1.0 %copy-done.4 = bf16[512,512]{1,0:T(8,128)(2,1)S(1)} copy-done((bf16[512,512]{1,0:T(8,128)(2,1)S(1)}, bf16[512,512]{1,0:T(8,128)(2,1)}, u32[]{:S(2)}) %copy-start.4) | copy-done | bytes 524312
  40.2 5.0 %shard_map.95 = (f32[5,8,16,129]{3,2,1,0:T(8,128)S(1)}, bf16[1,5,8,16,129]{4,3,2,1,0:T(8,128)(2,1)S(1)}) custom-call(s32[5]{0:T(128)S(1)} %stack.23.info, bf16[16,2176]{1,0:T(8,128)(2,1)S(1)} %constant_dynamic-update-slice_fusion.own, bf16[16,2176]{1,0:T(8,128)(2,1)S(1)} %collective-permute-done.27.part_0, ...), custom_call_target="tpu_custom_call" | custom-call | tf_op jit(solution)/shard_map/pallas_call | solution.py:196
  45.2 2.3 %collective-permute-start.29 = (bf16[5,8,16,129]{3,2,1,0:T(8,128)(2,1)S(1)}, bf16[5,8,16,129]{3,2,1,0:T(8,128)(2,1)S(1)}, u32[]{:S(2)}, u32[]{:S(2)}) collective-permute-start(bf16[5,8,16,129]{3,2,1,0:T(8,128)(2,1)S(1)} %bitcast.14), channel_id=1, source_target_pairs={{0,1},{1,0},{2,3},{3,2},{4,5},{5,4},{6,7},{7,6},{8,9},{9,8},{10,11... | collective-permute-start | bytes 495368 | tf_op jit(solution)/shard_map/ppermute | solution.py:253
  47.5 6.7 %collective-permute-done.29 = bf16[5,8,16,129]{3,2,1,0:T(8,128)(2,1)S(1)} collective-permute-done((bf16[5,8,16,129]{3,2,1,0:T(8,128)(2,1)S(1)}, bf16[5,8,16,129]{3,2,1,0:T(8,128)(2,1)S(1)}, u32[]{:S(2)}, u32[]{:S(2)}) %collective-permute-start.29) | collective-permute-done | bytes 165152 | tf_op jit(solution)/shard_map/ppermute | solution.py:253
  54.3 0.1 convert_add_fusion
  54.4 0.7 %slice_bitcast_fusion = f32[8,16,129]{2,1,0:T(8,128)} fusion(f32[5,8,16,129]{3,2,1,0:T(8,128)S(1)} %convert_add_fusion), kind=kLoop, calls=%fused_computation.1 | loop fusion | bytes 132096 | tf_op jit(solution)/shard_map/squeeze | solution.py:254
  55.0 0.8 %slice.29 = f32[4,8,16,129]{3,2,1,0:T(8,128)} slice(f32[5,8,16,129]{3,2,1,0:T(8,128)S(1)} %convert_add_fusion), slice={[1:5], [0:8], [0:16], [0:129]} | slice | bytes 528384 | tf_op jit(solution)/shard_map/slice | solution.py:254
  (2 shorter events, 0.0 us)
Async XLA Ops:
  1.3 6.1 %collective-permute-start.26 = (bf16[16,128]{1,0:T(8,128)(2,1)S(1)}, bf16[16,128]{1,0:T(8,128)(2,1)S(1)}, u32[]{:S(2)}, u32[]{:S(2)}) collective-permute-start(bf16[16,128]{1,0:T(8,128)(2,1)S(1)} %slice.25), channel_id=1, source_target_pairs={{0,1},{2,3},{4,5},{6,7},{8,9},{10,11},{12,13},{14,15},{16,17},{18,... | collective-permute-start | bytes 12296 | tf_op jit(solution)/shard_map/ppermute | solution.py:226
  7.5 5.5 %copy-start.5 = (s32[4]{0:T(128)S(1)}, s32[4]{0:T(128)}, u32[]{:S(2)}) copy-start(s32[4]{0:T(128)} %param.36) | copy-start | bytes 52
  8.3 26.7 %collective-permute-start.28 = (bf16[16,2176]{1,0:T(8,128)(2,1)S(1)}, bf16[16,2176]{1,0:T(8,128)(2,1)S(1)}, u32[]{:S(2)}, u32[]{:S(2)}) collective-permute-start(bf16[16,2176]{1,0:T(8,128)(2,1)S(1)} %constant_dynamic-update-slice_fusion.own), channel_id=1, source_target_pairs={{0,30},{2,28},{4,26},{6,24},{8,22},{10,20},{12,18},{14,16},{16,14}... | collective-permute-start | bytes 208904 | tf_op jit(solution)/shard_map/ppermute | solution.py:219
  11.5 23.5 %collective-permute-start.27 = (bf16[16,2176]{1,0:T(8,128)(2,1)S(1)}, bf16[16,2176]{1,0:T(8,128)(2,1)S(1)}, u32[]{:S(2)}, u32[]{:S(2)}) collective-permute-start(bf16[16,2176]{1,0:T(8,128)(2,1)S(1)} %constant_dynamic-update-slice_fusion.own), channel_id=1, source_target_pairs={{0,2},{2,0},{4,6},{6,4},{8,10},{10,8},{12,14},{14,12},{16,18},{18,... | collective-permute-start | bytes 208904 | tf_op jit(solution)/shard_map/ppermute | solution.py:219
  23.3 0.7 %copy-start.6 = (f32[96]{0:T(128)S(1)}, f32[96]{0:T(128)}, u32[]{:S(2)}) copy-start(f32[96]{0:T(128)} %param.35) | copy-start | bytes 1156
  24.0 6.2 %collective-permute-start.23 = (bf16[16,2176]{1,0:T(8,128)(2,1)S(1)}, bf16[16,2176]{1,0:T(8,128)(2,1)}, u32[]{:S(2)}, u32[]{:S(2)}) collective-permute-start(bf16[16,2176]{1,0:T(8,128)(2,1)S(1)} %param.23), channel_id=1, source_target_pairs={{0,24},{2,26},{4,28},{6,30},{8,16},{10,18},{12,20},{14,22},{16,8},... | collective-permute-start | bytes 208904 | tf_op jit(solution)/shard_map/cond/branch_10_fun/ppermute | solution.py:219
  30.3 4.7 %collective-permute-start.5 = (bf16[16,2176]{1,0:T(8,128)(2,1)S(1)}, bf16[16,2176]{1,0:T(8,128)(2,1)}, u32[]{:S(2)}, u32[]{:S(2)}) collective-permute-start(bf16[16,2176]{1,0:T(8,128)(2,1)S(1)} %param.5), channel_id=1, source_target_pairs={{0,14},{2,12},{4,10},{6,8},{8,6},{10,4},{12,2},{14,0},{16,30},{18,... | collective-permute-start | bytes 208904 | tf_op jit(solution)/shard_map/cond/branch_5_fun/ppermute | solution.py:219
  35.0 1.0 %copy-start = (bf16[1024,256]{1,0:T(8,128)(2,1)S(1)}, bf16[1024,256]{1,0:T(8,128)(2,1)}, u32[]{:S(2)}) copy-start(bf16[1024,256]{1,0:T(8,128)(2,1)} %constant.38.clone.lag_table) | copy-start | bytes 1572868
  36.1 1.0 %copy-start.1 = (bf16[512,512]{1,0:T(8,128)(2,1)S(1)}, bf16[512,512]{1,0:T(8,128)(2,1)}, u32[]{:S(2)}) copy-start(bf16[512,512]{1,0:T(8,128)(2,1)} %constant.37.clone.odd_lo) | copy-start | bytes 1572868
  37.1 1.0 %copy-start.2 = (bf16[512,512]{1,0:T(8,128)(2,1)S(1)}, bf16[512,512]{1,0:T(8,128)(2,1)}, u32[]{:S(2)}) copy-start(bf16[512,512]{1,0:T(8,128)(2,1)} %constant.36.clone.odd_hi) | copy-start | bytes 1572868
  38.1 1.0 %copy-start.3 = (bf16[512,512]{1,0:T(8,128)(2,1)S(1)}, bf16[512,512]{1,0:T(8,128)(2,1)}, u32[]{:S(2)}) copy-start(bf16[512,512]{1,0:T(8,128)(2,1)} %constant.35.clone.even_lo) | copy-start | bytes 1572868
  39.2 1.0 %copy-start.4 = (bf16[512,512]{1,0:T(8,128)(2,1)S(1)}, bf16[512,512]{1,0:T(8,128)(2,1)}, u32[]{:S(2)}) copy-start(bf16[512,512]{1,0:T(8,128)(2,1)} %constant.34.clone.even_hi) | copy-start | bytes 1572868
  45.2 9.1 %collective-permute-start.29 = (bf16[5,8,16,129]{3,2,1,0:T(8,128)(2,1)S(1)}, bf16[5,8,16,129]{3,2,1,0:T(8,128)(2,1)S(1)}, u32[]{:S(2)}, u32[]{:S(2)}) collective-permute-start(bf16[5,8,16,129]{3,2,1,0:T(8,128)(2,1)S(1)} %bitcast.14), channel_id=1, source_target_pairs={{0,1},{1,0},{2,3},{3,2},{4,5},{5,4},{6,7},{7,6},{8,9},{9,8},{10,11... | collective-permute-start | bytes 495368 | tf_op jit(solution)/shard_map/ppermute | solution.py:253
